TPU v7x, 32 devices: a whole 2x2x4 slice. The times are simulated.
32 devices in a mesh: segment: 2 (over x), owner: 16 (over z, y, core).
Axes of the slice: x: 2, y: 2, z: 4, core: 2. Of those that a mesh axis runs over, the one named last changes fastest.
Arguments:
- layer_input_rows: bfloat16 [2, 2048, 4096], P('segment', 'owner'), may hold values from -6 to 6
- output_gradient: bfloat16 [2, 2048, 1024], P('segment', 'owner'), may hold values from -6 to 6
- tenant: int32 [2048, 1], P('owner'), may hold values from 0 to 15; in each aligned block of 128 rows (0 to 127, 128 to 255, ...) at most 16 rows name the same one
- adapter_owner_index: int32 [16], replicated, may hold values from 0 to 15, each once
- adapter_down_weight: bfloat16 [2, 16, 4096, 64], P('segment', 'owner'), may hold values from -0.09375 to 0.09375
- adapter_up_weight: bfloat16 [2, 16, 64, 1024], P('segment', 'owner'), may hold values from -0.1875 to 0.1875
Outputs:
- passed_grad: bfloat16 [2, 2048, 4096], P('segment', 'owner')
- grad_down: float32 [2, 16, 4096, 64], P('segment', 'owner')
- grad_up: float32 [2, 16, 64, 1024], P('segment', 'owner')
Inputs may be any that keep to these rules, and one draw needn't show every extreme that they name: `tenant`: within the rows of one device no adapter is named by more than 16 rows, and in every draw some device names some adapter exactly 16 times. `adapter_owner_index`: each owner index appears once.
All inputs are finite; a program needn't handle non-finite values.
Results may differ from a plain program's by a relative error of at most 0.014.
Values may be sent and summed in bfloat16 or wider, within the bound.
A program may use at most 128 MiB of HBM per device.

v0:
```python
import jax
import jax.numpy as jnp
from jax import lax
from jax.sharding import PartitionSpec as P

adapter_scale = 2.0


def prefix(x, axis, join, neutral):
    count = lax.axis_size(axis)
    place = lax.axis_index(axis)
    ahead = count - 1 - place
    gathered = lax.all_gather(x.astype(jnp.bfloat16), axis)
    state = jnp.zeros_like(x) + jnp.asarray(neutral, x.dtype)

    def one(step, state):
        source = count - 1 - step
        return join(state, lax.dynamic_index_in_dim(gathered, source, 0, False).astype(x.dtype))

    return lax.fori_loop(0, ahead, one, state)


def local(
    layer_input_rows,
    output_gradient,
    tenant,
    adapter_owner_index,
    adapter_down_weight,
    adapter_up_weight,
):
    inputs = layer_input_rows[0]
    gradient_list = output_gradient[0]
    tok_rows = inputs.shape[0]
    width = inputs.shape[1]
    out_width = gradient_list.shape[1]
    owners = lax.axis_size("owner")
    capacity = 2 * tok_rows // owners
    highest_precision = lax.Precision.HIGHEST
    ids = tenant[:, 0]
    adapter_count = adapter_owner_index.shape[0]
    matched = ids[:, None] == jnp.arange(adapter_count, dtype=jnp.int32)[None, :]
    dest = jnp.sum(jnp.where(matched, adapter_owner_index[None, :], 0), axis=1)
    onehot = (dest[:, None] == jnp.arange(owners, dtype=jnp.int32)[None, :]).astype(jnp.int32)
    rank = jnp.sum((jnp.cumsum(onehot, axis=0) - 1) * onehot, axis=1)
    target = dest * capacity + rank
    placing = (jnp.arange(owners * capacity, dtype=jnp.int32)[:, None] == target[None, :]).astype(
        jnp.bfloat16
    )
    send_inputs = jnp.dot(placing, inputs, preferred_element_type=jnp.float32).astype(jnp.bfloat16)
    send_grads = jnp.dot(placing, gradient_list, preferred_element_type=jnp.float32).astype(
        jnp.bfloat16
    )
    send_inputs = send_inputs.reshape(owners, capacity, width)
    send_grads = send_grads.reshape(owners, capacity, out_width)
    down_factor = adapter_down_weight[0, 0]
    up_factor = adapter_up_weight[0, 0]
    recv_inputs, recv_grads = (
        lax.all_to_all(send_inputs, "owner", split_axis=0, concat_axis=0, tiled=True),
        lax.all_to_all(send_grads, "owner", split_axis=0, concat_axis=0, tiled=True),
    )
    rows_in = recv_inputs.reshape(owners * capacity, width)
    rows_grad = recv_grads.reshape(owners * capacity, out_width)
    scale_weight = adapter_scale * jnp.einsum(
        "rm,km->rk", rows_grad, up_factor, preferred_element_type=jnp.float32
    )
    partial_terms = jnp.einsum(
        "rk,dk->rd",
        scale_weight,
        down_factor,
        precision=highest_precision,
        preferred_element_type=jnp.float32,
    )
    partial_terms = partial_terms.astype(jnp.bfloat16).reshape(owners, capacity, width)
    returned = lax.all_to_all(partial_terms, "owner", split_axis=0, concat_axis=0, tiled=True)
    projected_rows = jnp.dot(rows_in, down_factor, preferred_element_type=jnp.float32)
    grad_down = jnp.einsum(
        "rd,rk->dk",
        rows_in,
        scale_weight,
        precision=highest_precision,
        preferred_element_type=jnp.float32,
    )
    grad_up = jnp.einsum(
        "rk,rm->km",
        projected_rows,
        rows_grad,
        precision=highest_precision,
        preferred_element_type=jnp.float32,
    )
    own_term = jnp.einsum(
        "sr,sd->rd",
        placing,
        returned.reshape(owners * capacity, width),
        preferred_element_type=jnp.float32,
    )

    def combine(earlier, later):
        return earlier + later

    above = prefix(own_term, "segment", combine, jnp.zeros_like(own_term))
    passed = (above + own_term).astype(jnp.bfloat16)
    return (passed[None], grad_down[None, None], grad_up[None, None])


def solution(mesh):
    return jax.shard_map(
        local,
        mesh=mesh,
        in_specs=(
            P("segment", "owner", None),
            P("segment", "owner", None),
            P("owner", None),
            P(),
            P("segment", "owner", None, None),
            P("segment", "owner", None, None),
        ),
        out_specs=(
            P("segment", "owner", None),
            P("segment", "owner", None, None),
            P("segment", "owner", None, None),
        ),
        check_vma=False,
    )
```

profile of v0, /device:TPU:13, one launch (start us, length us, event | category | flops | bytes accessed | tf_op | source)
XLA Modules:
  0.0 156.8 jit_solution(6763170391971825095)
XLA Ops:
  7.2 0.0 copy-start
  7.2 0.0 copy-start.5
  7.2 0.0 copy-start.4
  7.2 1.0 select_reduce_fusion.1
  8.2 0.1 fusion.11
  8.3 0.2 reduce_window_sum.11
  8.4 0.2 select_reduce_fusion
  8.6 1.2 convolution_convert_fusion.2
  9.9 19.9 %all_to_all.15 = bf16[16,16,1024]{2,1,0:T(8,128)(2,1)S(1)} all-to-all(bf16[16,16,1024]{2,1,0:T(8,128)(2,1)S(1)} %bitcast.49), channel_id=1, replica_groups=mesh['segment'=2,'owner'=16] {'owner'}, dimensions={0} | all-to-all | bytes 1048576 | tf_op jit(solution)/shard_map/all_to_all | solution.py:59
  29.8 0.0 copy-start.2
  29.8 0.8 copy-done.2
  30.6 0.0 copy-done.5
  30.6 0.3 convolution_multiply_fusion
  30.9 0.0 copy-done.4
  30.9 3.2 %convolution_convert_fusion.1 = bf16[256,4096]{1,0:T(8,128)(2,1)} fusion(f32[256,64]{0,1:T(8,128)S(1)} %convolution_multiply_fusion, bf16[1,1,4096,64]{2,3,1,0:T(8,128)(2,1)S(1)} %copy-done.4), kind=kOutput, calls=%fused_computation.2 | convolution fusion | flops 806354944 | bytes 2686976 | tf_op jit(solution)/shard_map/rk,dk->rd/dot_general | solution.py:66
  34.1 5.0 %all-to-all-start.1 = ((bf16[16,16,4096]{2,1,0:T(8,128)(2,1)}), bf16[16,16,4096]{2,1,0:T(8,128)(2,1)S(1)}, u32[]{:S(2)}, u32[]{:S(2)}) async-start(bf16[16,16,4096]{2,1,0:T(8,128)(2,1)} %bitcast.46), calls=%async_computation.1 | async-start | bytes 4194304 | tf_op jit(solution)/shard_map/all_to_all | solution.py:74
  39.1 0.0 copy-done
  39.1 2.0 %convolution_convert_fusion = bf16[256,4096]{1,0:T(8,128)(2,1)} fusion(bf16[1,128,4096]{2,1,0:T(8,128)(2,1)S(1)} %copy-done, s32[128]{0:T(128)S(1)} %multiply_add_fusion), kind=kOutput, calls=%fused_computation.1 | convolution fusion | flops 269516800 | bytes 3146240 | tf_op jit(solution)/shard_map/dot_general | solution.py:49
  41.1 45.4 %all-to-all-done.1 = bf16[16,16,4096]{2,1,0:T(8,128)(2,1)S(1)} async-done(((bf16[16,16,4096]{2,1,0:T(8,128)(2,1)}), bf16[16,16,4096]{2,1,0:T(8,128)(2,1)S(1)}, u32[]{:S(2)}, u32[]{:S(2)}) %all-to-all-start.1) | async-done | bytes 2097184 | tf_op jit(solution)/shard_map/all_to_all | solution.py:74
  86.5 0.0 copy-start.1
  86.5 1.3 copy-done.1
  87.8 4.9 %all-to-all-start.2 = ((bf16[16,16,4096]{2,1,0:T(8,128)(2,1)}), bf16[16,16,4096]{2,1,0:T(8,128)(2,1)S(1)}, u32[]{:S(2)}, u32[]{:S(2)}) async-start(bf16[16,16,4096]{2,1,0:T(8,128)(2,1)} %bitcast.44), calls=%async_computation.2 | async-start | bytes 4194304 | tf_op jit(solution)/shard_map/all_to_all | solution.py:58
  92.7 0.0 all-gather.3.cloned.1.call-start
  92.8 3.7 %fusion.12 = (bf16[128,4096]{1,0:T(8,128)(2,1)}, f32[128,4096]{1,0:T(8,128)}) fusion(bf16[256,4096]{1,0:T(8,128)(2,1)} %bitcast.45, s32[128]{0:T(128)S(1)} %multiply_add_fusion), kind=kOutput, calls=%fused_computation.26 | convolution fusion | flops 268992512 | bytes 5243392 | tf_op jit(solution)/shard_map/sr,sd->rd/dot_general | solution.py:90
  96.5 0.0 all-gather.3.cloned.1.call-update
  96.6 43.6 %all-to-all-done.2 = bf16[16,16,4096]{2,1,0:T(8,128)(2,1)S(1)} async-done(((bf16[16,16,4096]{2,1,0:T(8,128)(2,1)}), bf16[16,16,4096]{2,1,0:T(8,128)(2,1)S(1)}, u32[]{:S(2)}, u32[]{:S(2)}) %all-to-all-start.2) | async-done | bytes 2097184 | tf_op jit(solution)/shard_map/all_to_all | solution.py:58
  140.1 0.0 copy-start.3
  140.1 1.8 %fusion.2 = f32[256,64]{1,0:T(8,128)S(1)} fusion(bf16[256,4096]{1,0:T(8,128)(2,1)S(1)} %bitcast.41, bf16[1,1,4096,64]{2,3,1,0:T(8,128)(2,1)} %param.12), kind=kOutput, calls=%fused_computation.10 | convolution fusion | flops 134217728 | bytes 2686976 | tf_op jit(solution)/shard_map/dot_general | solution.py:75
  141.9 0.0 copy-done.3
  142.0 1.1 convolution_bitcast_fusion.1
  143.1 2.2 %convolution_bitcast_fusion = f32[1,1,4096,64]{2,3,1,0:T(8,128)} fusion(bf16[256,4096]{1,0:T(8,128)(2,1)S(1)} %bitcast.42, f32[256,64]{0,1:T(8,128)S(1)} %convolution_multiply_fusion), kind=kOutput, calls=%fused_computation.3 | convolution fusion | flops 805306368 | bytes 3211264 | tf_op jit(solution)/shard_map/rd,rk->dk/dot_general | solution.py:76
  145.3 0.0 all-gather.3.cloned.1.call-done
  145.3 0.2 broadcast_in_dim.30
  145.5 1.7 %while.12 = (s32[]{:T(128)}, f32[128,4096]{1,0:T(8,128)S(1)}, s32[]{:T(128)}, bf16[2,128,4096]{2,1,0:T(8,128)(2,1)}, s32[]{:T(128)}, /*index=5*/s32[]{:T(128)}, s32[]{:T(128)}) while((s32[]{:T(128)}, f32[128,4096]{1,0:T(8,128)S(1)}, s32[]{:T(128)}, bf16[2,128,4096]{2,1,0:T(8,128)(2,1)}, s32[]{:T(128)}, /*index=5*/s32[]{:T(128)}, ...), condition=%wide.region_4.5_spmd, body=%wide.region_3.4_spmd.sunk | while | flops 1048582 | bytes 5243007 | solution.py:20
  145.5 1.7 %convert_add_fusion.2 = f32[128,4096]{1,0:T(8,128)S(1)} fusion(f32[128,4096]{1,0:T(8,128)S(1)} %get-tuple-element.104, bf16[2,128,4096]{2,1,0:T(8,128)(2,1)} %get-tuple-element.113, s32[]{:T(128)S(6)} %select_n.14), kind=kLoop, calls=%fused_computation.clone.1 | loop fusion | flops 1048576 | bytes 5242884 | tf_op jit(solution)/shard_map/while/body/add | solution.py:98
  147.2 2.8 %fusion = bf16[1,128,4096]{2,1,0:T(8,128)(2,1)} fusion(f32[128,4096]{1,0:T(8,128)S(1)} %get-tuple-element.59, f32[128,4096]{1,0:T(8,128)} %get-tuple-element.69), kind=kLoop, calls=%fused_computation.8 | loop fusion | flops 1048576 | bytes 5242880 | tf_op jit(solution)/shard_map/broadcast_in_dim | solution.py:102
  (1 shorter events, 0.0 us)
Async XLA Ops:
  7.2 31.9 %copy-start = (bf16[1,128,4096]{2,1,0:T(8,128)(2,1)S(1)}, bf16[1,128,4096]{2,1,0:T(8,128)(2,1)}, u32[]{:S(2)}) copy-start(bf16[1,128,4096]{2,1,0:T(8,128)(2,1)} %param.8) | copy-start | bytes 3145732
  7.2 23.4 %copy-start.5 = (bf16[1,1,64,1024]{3,2,1,0:T(8,128)(2,1)S(1)}, bf16[1,1,64,1024]{3,2,1,0:T(8,128)(2,1)}, u32[]{:S(2)}) copy-start(bf16[1,1,64,1024]{3,2,1,0:T(8,128)(2,1)} %param.13) | copy-start | bytes 393220
  7.2 23.7 %copy-start.4 = (bf16[1,1,4096,64]{2,3,1,0:T(8,128)(2,1)S(1)}, bf16[1,1,4096,64]{2,3,1,0:T(8,128)(2,1)}, u32[]{:S(2)}) copy-start(bf16[1,1,4096,64]{2,3,1,0:T(8,128)(2,1)} %param.12) | copy-start | bytes 1572868
  29.8 0.8 copy-start.2
  34.1 52.4 %all-to-all-start.1 = ((bf16[16,16,4096]{2,1,0:T(8,128)(2,1)}), bf16[16,16,4096]{2,1,0:T(8,128)(2,1)S(1)}, u32[]{:S(2)}, u32[]{:S(2)}) async-start(bf16[16,16,4096]{2,1,0:T(8,128)(2,1)} %bitcast.46), calls=%async_computation.1 | async-start | bytes 4194304 | tf_op jit(solution)/shard_map/all_to_all | solution.py:74
  86.5 1.3 copy-start.1
  87.8 52.3 %all-to-all-start.2 = ((bf16[16,16,4096]{2,1,0:T(8,128)(2,1)}), bf16[16,16,4096]{2,1,0:T(8,128)(2,1)S(1)}, u32[]{:S(2)}, u32[]{:S(2)}) async-start(bf16[16,16,4096]{2,1,0:T(8,128)(2,1)} %bitcast.44), calls=%async_computation.2 | async-start | bytes 4194304 | tf_op jit(solution)/shard_map/all_to_all | solution.py:58
  92.7 52.5 %all-gather.3.cloned.1.call-start = ((), (), s32[]{:S(2)}) async-start(), calls=%async_computation.3 | async-start | bytes 3145728 | tf_op jit(solution)/shard_map/all_gather | solution.py:13
  140.1 1.8 %copy-start.3 = (bf16[16,16,1024]{2,1,0:T(8,128)(2,1)S(1)}, bf16[16,16,1024]{2,1,0:T(8,128)(2,1)}, u32[]{:S(2)}) copy-start(bf16[16,16,1024]{2,1,0:T(8,128)(2,1)} %copy-done.2) | copy-start | bytes 1572868
Sparse Core Ops, SparseCore 0:
  96.7 33.6 all-gather.2
where the time goes:
time: 157 us
  waiting for transfers between devices  89 us (57%)
  blocking collectives  19.9 us (13%)
  matrix products  15.6 us (10%)
  between operations  14.1 us (9%)
  starting transfers between devices  9.93 us (6%)
  other arithmetic  5.86 us (4%)
  local copies, waits for them, and re-layouts  2.32 us (1%)
    all_to_all x1, waiting for transfers between devices, local(): lax.all_to_all(partial_terms, 'owner', split_axis=0, concat_axis=0, tiled...  45.4 us
    all_to_all x1, waiting for transfers between devices, local(): lax.all_to_all(send_inputs, 'owner', split_axis=0, concat_axis=0, tiled=T...  43.6 us
    all_to_all x1, blocking collectives, local(): lax.all_to_all(send_grads, 'owner', split_axis=0, concat_axis=0, tiled=True)  19.9 us
    all_to_all x1, starting transfers between devices, local(): lax.all_to_all(partial_terms, 'owner', split_axis=0, concat_axis=0, tiled...  4.98 us
    all_to_all x1, starting transfers between devices, local(): lax.all_to_all(send_inputs, 'owner', split_axis=0, concat_axis=0, tiled=T...  4.91 us
    dot_general x1, matrix products, local(): jnp.einsum('sr,sd->rd', placing, returned.reshape(owners * capacity, widt...  3.75 us
    dot_general x1, matrix products, local(): jnp.einsum('rk,dk->rd', scale_weight, down_factor, precision=highest_prec...  3.2 us
  transfers between devices with their start and end apart: 3, of which 2 were waited for; matrix products, arithmetic and copies ran while one was open for 7% of the time, Pallas kernels for 0%

commit v1 on v0

--- a/solution.py
+++ b/solution.py
@@ -1,6 +1,10 @@
+import functools
+
 import jax
 import jax.numpy as jnp
 from jax import lax
+from jax.experimental import pallas as pl
+from jax.experimental.pallas import tpu as pltpu
 from jax.sharding import PartitionSpec as P
 
 adapter_scale = 2.0
@@ -102,9 +106,360 @@
     return (passed[None], grad_down[None, None], grad_up[None, None])
 
 
+lines = 4
+plane = 4
+chunks = 2
+bf16 = jnp.bfloat16
+f32 = jnp.float32
+
+
+def dot_nt(a, b):
+    return lax.dot_general(a, b, (((1,), (1,)), ((), ())), preferred_element_type=f32)
+
+
+def dot_nn(a, b):
+    return jnp.dot(a, b, preferred_element_type=f32)
+
+
+def lines_kernel(
+    x, g, ids, owner_of, a, b,
+    passed, gd, gu,
+    sx, sg, rx, rg, at, bt, a1, cf, cft, c1, ts, tr, sl, sr, ql, qr, ul, ur, vl, vr, gup,
+    x_s, x_r, g_s, g_r, a_s, a_r, b_s, b_r, a1_s, a1_r, c_s, c_r, t_s, t_r, d_s, d_r, u_s, u_r,
+):
+    tok, width = x.shape
+    out_width = g.shape[1]
+    part = width // chunks
+    cap = sx.shape[3]
+    rank_dim = b.shape[0]
+    rows = plane * cap
+    seg = lax.axis_index("segment")
+    own = lax.axis_index("owner")
+    z = own // plane
+    h = own % plane
+    upper = seg == 1
+    lower = seg == 0
+    pending = []
+
+    def signal(segment, owner):
+        pl.semaphore_signal(
+            barrier, inc=1, device_id=(segment, owner), device_id_type=pl.DeviceIdType.MESH
+        )
+
+    def copy(source, sink, send, recv, segment, owner):
+        return pltpu.make_async_remote_copy(
+            src_ref=source, dst_ref=sink, send_sem=send, recv_sem=recv,
+            device_id=(segment, owner), device_id_type=pl.DeviceIdType.MESH,
+        )
+
+    def go(cond, make):
+        if cond is None:
+            make().start()
+        else:
+            pl.when(cond)(lambda: make().start())
+        pending.append((cond, make))
+
+    def host(k):
+        return z * plane + (h + k) % plane
+
+    has_left = z > 0
+    has_right = z < lines - 1
+
+    barrier = pltpu.get_barrier_semaphore()
+    for k in range(1, plane):
+        signal(seg, host(k))
+    signal(1 - seg, own)
+    pl.when(has_left)(lambda: signal(seg, own - plane))
+    pl.when(has_right)(lambda: signal(seg, own + plane))
+
+    n_owner = lines * plane
+    n_adapter = owner_of.shape[0]
+    matched = lax.broadcasted_iota(jnp.int32, (n_adapter, tok), 0) == ids[...]
+    dest = jnp.sum(jnp.where(matched, owner_of[...], 0), axis=0, keepdims=True)
+    onehot = (lax.broadcasted_iota(jnp.int32, (n_owner, tok), 0) == dest).astype(f32)
+    earlier = (
+        lax.broadcasted_iota(jnp.int32, (tok, tok), 0)
+        < lax.broadcasted_iota(jnp.int32, (tok, tok), 1)
+    ).astype(f32)
+    count = dot_nn(onehot.astype(bf16), earlier.astype(bf16))
+    rank = jnp.sum(count * onehot, axis=0, keepdims=True).astype(jnp.int32)
+    target = (dest % plane) * (lines * cap) + (dest // plane) * cap + rank
+    placing32 = (
+        lax.broadcasted_iota(jnp.int32, (plane * lines * cap, tok), 0) == target
+    ).astype(f32)
+    placing = placing32.astype(bf16)
+    placing_t = placing32.T.astype(bf16)
+
+    at[z] = a[...]
+    bt[z] = b[...]
+    sg[...] = dot_nn(placing, g[...]).astype(bf16).reshape(plane, lines, cap, out_width)
+    pl.semaphore_wait(
+        barrier, plane + jnp.where(has_left, 1, 0) + jnp.where(has_right, 1, 0)
+    )
+
+    def shard_go(buf, send, recv, k):
+        go(
+            (z >= k) & has_right,
+            lambda: copy(buf.at[z - k], buf.at[z - k], send.at[0, k], recv.at[z - k], seg, own + plane),
+        )
+        go(
+            (z + k < lines) & has_left,
+            lambda: copy(buf.at[z + k], buf.at[z + k], send.at[1, k], recv.at[z + k], seg, own - plane),
+        )
+
+    def shard_wait(buf, send, recv, k):
+        pl.when(z >= k)(
+            lambda: copy(buf.at[z - k], buf.at[z - k], send.at[0, k], recv.at[z - k], seg, host(1)).wait_recv()
+        )
+        pl.when(z + k < lines)(
+            lambda: copy(buf.at[z + k], buf.at[z + k], send.at[1, k], recv.at[z + k], seg, host(1)).wait_recv()
+        )
+
+    def across(j):
+        return copy(at.at[j], a1.at[j], a1_s.at[j], a1_r.at[j], 0, own)
+
+    def a_step(k):
+        shard_wait(at, a_s, a_r, k)
+        if k < lines - 1:
+            shard_go(at, a_s, a_r, k)
+        go((z >= k) & upper, lambda: across(z - k))
+        go((z + k < lines) & upper, lambda: across(z + k))
+
+    def g_copy(k):
+        return copy(
+            sg.at[(h + k) % plane], rg.at[:, h], g_s.at[k - 1], g_r.at[k - 1], seg, host(k)
+        )
+
+    def x_copy(q, k):
+        return copy(
+            sx.at[q, (h + k) % plane], rx.at[q, :, h], x_s.at[q, k - 1], x_r.at[q, k - 1], seg, host(k)
+        )
+
+    shard_go(bt, b_s, b_r, 0)
+    for k in range(1, plane):
+        go(None, functools.partial(g_copy, k))
+    shard_go(at, a_s, a_r, 0)
+    go(upper, lambda: across(z))
+    rg[:, h] = sg[h]
+    for q in range(chunks):
+        sx[q] = (
+            dot_nn(placing, x[:, q * part : (q + 1) * part])
+            .astype(bf16)
+            .reshape(plane, lines, cap, part)
+        )
+        for k in range(1, plane):
+            go(None, functools.partial(x_copy, q, k))
+        rx[q, :, h] = sx[q, h]
+    for k in range(1, lines):
+        shard_wait(bt, b_s, b_r, k)
+        if k < lines - 1:
+            shard_go(bt, b_s, b_r, k)
+
+    cf[...] = jnp.zeros_like(cf)
+    for k in range(1, plane):
+        g_copy(k).wait_recv()
+    for j in range(lines):
+        grads = rg[j].reshape(rows, out_width)
+        cf[j, :, :rank_dim] = (adapter_scale * dot_nt(grads, bt[j])).astype(bf16)
+        cft[j, :, :rows] = (adapter_scale * dot_nt(bt[j], grads)).astype(bf16)
+
+    def coef_copy():
+        return copy(cf, c1, c_s, c_r, 0, own)
+
+    go(upper, coef_copy)
+    a_step(1)
+
+    def sums(value, cols, send_l, send_r, recv_l, recv_r, s_sem, r_sem):
+        def left(t):
+            return copy(send_l.at[t], recv_l.at[t], s_sem.at[0, t], r_sem.at[0, t], seg, own - plane)
+
+        def right(t):
+            return copy(send_r.at[t], recv_r.at[t], s_sem.at[1, t], r_sem.at[1, t], seg, own + plane)
+
+        for t in range(lines - 1):
+            for goal, buf, got, make, cond, more in (
+                (t, send_l, recv_l, left, z > t, has_right),
+                (lines - 1 - t, send_r, recv_r, right, z < lines - 1 - t, has_left),
+            ):
+                @pl.when(cond & jnp.logical_not(more))
+                def _():
+                    buf[goal] = value(goal).astype(bf16)
+
+                @pl.when(cond & more)
+                def _():
+                    mine = value(goal)
+                    make(goal).wait_recv()
+                    buf[goal] = (mine + got[goal].astype(f32)).astype(bf16)
+
+                go(cond, functools.partial(make, goal))
+
+        def finish(out):
+            out[:, cols] = value(z)
+
+            @pl.when(has_right)
+            def _():
+                left(z).wait_recv()
+                out[:, cols] += recv_l[z].astype(f32)
+
+            @pl.when(has_left)
+            def _():
+                right(z).wait_recv()
+                out[:, cols] += recv_r[z].astype(f32)
+
+        return finish
+
+    def down_sums(q):
+        for k in range(1, plane):
+            x_copy(q, k).wait_recv()
+        return sums(
+            lambda j: dot_nn(cft[j, :, :rows], rx[q, j].reshape(rows, part)),
+            pl.ds(q * part, part),
+            sl.at[q], sr.at[q], ql.at[q], qr.at[q], d_s.at[q], d_r.at[q],
+        )
+
+    order = (z, z + 1 - 2 * (z % 2), 2 - z // 2, 3 - 3 * (z // 2))
+
+    def t_copy(i, k):
+        return copy(
+            ts.at[order[i], (h + k) % plane], tr.at[h, order[i]],
+            t_s.at[i, k - 1], t_r.at[i, k - 1], seg, host(k),
+        )
+
+    def term(i):
+        j = order[i]
+        for q in range(chunks):
+            cols = pl.ds(q * part, part)
+            mine = dot_nn(cf[j, :, :rank_dim], at[j, :, cols]).astype(bf16)
+
+            @pl.when(upper)
+            def _():
+                ts[j, :, :, cols] = mine.reshape(plane, cap, part)
+
+            @pl.when(lower)
+            def _():
+                if q == 0:
+                    across(j).wait_recv()
+                above = dot_nn(c1[j, :, :rank_dim], a1[j, :, cols]).astype(bf16)
+                total = (mine.astype(f32) + above.astype(f32)).astype(bf16)
+                ts[j, :, :, cols] = total.reshape(plane, cap, part)
+
+        for k in range(1, plane):
+            go(None, functools.partial(t_copy, i, k))
+        tr[h, j] = ts[j, h]
+
+    def project(i):
+        j = order[i]
+        proj = jnp.zeros((rank_dim, rows), f32)
+        for q in range(chunks):
+            proj += dot_nt(at[j, :, q * part : (q + 1) * part], rx[q, j].reshape(rows, part))
+        gup[j] = dot_nn(proj.astype(bf16), rg[j].reshape(rows, out_width))
+
+    ends = [down_sums(0)]
+    pl.when(lower)(lambda: coef_copy().wait_recv())
+    term(0)
+    a_step(2)
+    ends.append(down_sums(1))
+    term(1)
+    project(0)
+    project(1)
+    a_step(3)
+    term(2)
+    project(2)
+    project(3)
+    up_end = sums(lambda j: gup[j], pl.ds(0, out_width), ul, ur, vl, vr, u_s, u_r)
+    term(3)
+    for end in ends:
+        end(gd)
+    up_end(gu)
+    for i in range(lines):
+        for k in range(1, plane):
+            t_copy(i, k).wait_recv()
+    for q in range(chunks):
+        cols = pl.ds(q * part, part)
+        passed[:, cols] = dot_nn(
+            placing_t, tr[:, :, :, cols].reshape(plane * lines * cap, part)
+        ).astype(bf16)
+    for cond, make in pending:
+        if cond is None:
+            make().wait_send()
+        else:
+            pl.when(cond)(functools.partial(lambda make: make().wait_send(), make))
+
+
+def local_lines(
+    layer_input_rows,
+    output_gradient,
+    tenant,
+    adapter_owner_index,
+    adapter_down_weight,
+    adapter_up_weight,
+):
+    x, g = layer_input_rows[0], output_gradient[0]
+    tok, width = x.shape
+    out_width = g.shape[1]
+    rank_dim = adapter_up_weight.shape[2]
+    cap = 2 * tok // (lines * plane)
+    rows = plane * cap
+    part = width // chunks
+    lanes = 128
+    vmem = pl.BlockSpec(memory_space=pltpu.VMEM)
+    dma = pltpu.SemaphoreType.DMA
+    passed, gd, gu = pl.pallas_call(
+        lines_kernel,
+        out_shape=(
+            jax.ShapeDtypeStruct((tok, width), bf16),
+            jax.ShapeDtypeStruct((rank_dim, width), f32),
+            jax.ShapeDtypeStruct((rank_dim, out_width), f32),
+        ),
+        in_specs=[vmem] * 6,
+        out_specs=(vmem,) * 3,
+        scratch_shapes=[
+            pltpu.VMEM((chunks, plane, lines, cap, part), bf16),
+            pltpu.VMEM((plane, lines, cap, out_width), bf16),
+            pltpu.VMEM((chunks, lines, plane, cap, part), bf16),
+            pltpu.VMEM((lines, plane, cap, out_width), bf16),
+            pltpu.VMEM((lines, rank_dim, width), bf16),
+            pltpu.VMEM((lines, rank_dim, out_width), bf16),
+            pltpu.VMEM((lines, rank_dim, width), bf16),
+            pltpu.VMEM((lines, rows, lanes), bf16),
+            pltpu.VMEM((lines, rank_dim, lanes), bf16),
+            pltpu.VMEM((lines, rows, lanes), bf16),
+            pltpu.VMEM((lines, plane, cap, width), bf16),
+            pltpu.VMEM((plane, lines, cap, width), bf16),
+        ]
+        + [pltpu.VMEM((chunks, lines, rank_dim, part), bf16)] * 4
+        + [pltpu.VMEM((lines, rank_dim, out_width), bf16)] * 4
+        + [
+            pltpu.VMEM((lines, rank_dim, out_width), f32),
+            dma((chunks, plane - 1)), dma((chunks, plane - 1)),
+            dma((plane - 1,)), dma((plane - 1,)),
+            dma((2, lines)), dma((lines,)),
+            dma((2, lines)), dma((lines,)),
+            dma((lines,)), dma((lines,)),
+            dma, dma,
+            dma((lines, plane - 1)), dma((lines, plane - 1)),
+            dma((chunks, 2, lines)), dma((chunks, 2, lines)),
+            dma((2, lines)), dma((2, lines)),
+        ],
+        compiler_params=pltpu.CompilerParams(
+            collective_id=0, has_side_effects=True, vmem_limit_bytes=56 * 1024 * 1024
+        ),
+        name="adapter_lines",
+    )(
+        x,
+        g,
+        tenant.reshape(1, tok),
+        adapter_owner_index.reshape(-1, 1),
+        adapter_down_weight[0, 0].T,
+        adapter_up_weight[0, 0],
+    )
+    return (passed[None], gd.T[None, None], gu[None, None])
+
+
 def solution(mesh):
+    planned = mesh.shape["segment"] == 2 and mesh.shape["owner"] == lines * plane
     return jax.shard_map(
-        local,
+        local_lines if planned else local,
         mesh=mesh,
         in_specs=(
             P("segment", "owner", None),

time: 157 us -> 93.4 us (0.59)
  the two profiles are of different devices: /device:TPU:13 before, /device:TPU:17 now
where the time goes in v1:
time: 93.4 us; the launch traced here: 93.1 us
  Pallas kernels  87 us (93%)
  local copies, waits for them, and re-layouts  5.5 us (6%)
    pallas_call x1, Pallas kernels, local_lines(): pl.pallas_call(lines_kernel, out_shape=(jax.ShapeDtypeStruct((tok, width)...  87 us
    unnamed x9, local copies, waits for them, and re-layouts  4.82 us

profile of v1, /device:TPU:17, one launch (start us, length us, event | category | flops | bytes accessed | tf_op | source)
XLA Modules:
  0.0 93.1 jit_solution(10048104201678850321)
XLA Ops:
  0.6 0.0 copy-start.2
  0.6 0.6 copy-done.2
  1.3 0.7 copy.9.owner_of
  2.0 87.0 %adapter_lines.1 = (bf16[128,4096]{1,0:T(8,128)(2,1)}, f32[64,4096]{1,0:T(8,128)}, f32[64,1024]{1,0:T(8,128)}) custom-call(bf16[128,4096]{1,0:T(8,128)(2,1)} %bitcast.13, bf16[128,1024]{1,0:T(8,128)(2,1)} %bitcast.17, s32[1,128]{1,0:T(1,128)} %bitcast.20, s32[16,1]{1,0:T(8,128)} %copy.9.owner_of, bf16[64,4096]{1,0:T(8,128)(2,1)} %bitcast.16, ...), custom_call_target="tpu_custom_call" | custom-call | tf_op jit(solution)/shard_map/adapter_lines/pallas_call | solution.py:407
  89.0 0.0 copy-start
  89.0 2.4 %copy.13 = bf16[1,128,4096]{2,1,0:T(8,128)(2,1)} copy(bf16[1,128,4096]{2,1,0:T(8,128)(2,1)} %bitcast.15) | data formatting | bytes 2097152
  91.3 0.0 copy-done
  91.3 0.0 copy-start.1
  91.3 1.0 %copy.14 = f32[1,1,4096,64]{2,3,1,0:T(8,128)} copy(f32[1,1,4096,64]{2,3,1,0:T(8,128)S(1)} %bitcast.14) | data formatting | bytes 2097152
  92.3 0.1 copy-done.1
  92.4 0.7 copy.15
Async XLA Ops:
  0.6 0.7 copy-start.2
  89.0 2.4 %copy-start = (f32[64,4096]{1,0:T(8,128)S(1)}, f32[64,4096]{1,0:T(8,128)}, u32[]{:S(2)}) copy-start(f32[64,4096]{1,0:T(8,128)} %get-tuple-element.7) | copy-start | bytes 3145732
  91.3 1.1 %copy-start.1 = (f32[64,1024]{1,0:T(8,128)S(1)}, f32[64,1024]{1,0:T(8,128)}, u32[]{:S(2)}) copy-start(f32[64,1024]{1,0:T(8,128)} %get-tuple-element.8) | copy-start | bytes 786436

commit v2 on v1

--- a/solution.py
+++ b/solution.py
@@ -108,7 +108,8 @@
 
 lines = 4
 plane = 4
-chunks = 2
+chunks = 4
+parts = 2
 bf16 = jnp.bfloat16
 f32 = jnp.float32
 
@@ -130,6 +131,7 @@
     tok, width = x.shape
     out_width = g.shape[1]
     part = width // chunks
+    wide = width // parts
     cap = sx.shape[3]
     rank_dim = b.shape[0]
     rows = plane * cap
@@ -173,9 +175,12 @@
     pl.when(has_right)(lambda: signal(seg, own + plane))
 
     n_owner = lines * plane
-    n_adapter = owner_of.shape[0]
+    n_adapter = owner_of.shape[1]
+    square = (n_adapter, n_adapter)
+    diagonal = lax.broadcasted_iota(jnp.int32, square, 0) == lax.broadcasted_iota(jnp.int32, square, 1)
+    owner_column = jnp.sum(jnp.where(diagonal, owner_of[...], 0), axis=1, keepdims=True)
     matched = lax.broadcasted_iota(jnp.int32, (n_adapter, tok), 0) == ids[...]
-    dest = jnp.sum(jnp.where(matched, owner_of[...], 0), axis=0, keepdims=True)
+    dest = jnp.sum(jnp.where(matched, owner_column, 0), axis=0, keepdims=True)
     onehot = (lax.broadcasted_iota(jnp.int32, (n_owner, tok), 0) == dest).astype(f32)
     earlier = (
         lax.broadcasted_iota(jnp.int32, (tok, tok), 0)
@@ -190,8 +195,9 @@
     placing = placing32.astype(bf16)
     placing_t = placing32.T.astype(bf16)
 
-    at[z] = a[...]
     bt[z] = b[...]
+    for p in range(parts):
+        at[p, z] = a[:, p * wide : (p + 1) * wide]
     sg[...] = dot_nn(placing, g[...]).astype(bf16).reshape(plane, lines, cap, out_width)
     pl.semaphore_wait(
         barrier, plane + jnp.where(has_left, 1, 0) + jnp.where(has_right, 1, 0)
@@ -215,15 +221,24 @@
             lambda: copy(buf.at[z + k], buf.at[z + k], send.at[1, k], recv.at[z + k], seg, host(1)).wait_recv()
         )
 
-    def across(j):
-        return copy(at.at[j], a1.at[j], a1_s.at[j], a1_r.at[j], 0, own)
-
-    def a_step(k):
-        shard_wait(at, a_s, a_r, k)
+    def across(p, j):
+        return copy(at.at[p, j], a1.at[p, j], a1_s.at[p, j], a1_r.at[p, j], 0, own)
+
+    def a_start(p):
+        shard_go(at.at[p], a_s.at[p], a_r.at[p], 0)
+        go(upper, lambda: across(p, z))
+
+    def a_step(k, p):
+        shard_wait(at.at[p], a_s.at[p], a_r.at[p], k)
         if k < lines - 1:
-            shard_go(at, a_s, a_r, k)
-        go((z >= k) & upper, lambda: across(z - k))
-        go((z + k < lines) & upper, lambda: across(z + k))
+            shard_go(at.at[p], a_s.at[p], a_r.at[p], k)
+        go((z >= k) & upper, lambda: across(p, z - k))
+        go((z + k < lines) & upper, lambda: across(p, z + k))
+
+    def b_step(k):
+        shard_wait(bt, b_s, b_r, k)
+        if k < lines - 1:
+            shard_go(bt, b_s, b_r, k)
 
     def g_copy(k):
         return copy(
@@ -238,8 +253,6 @@
     shard_go(bt, b_s, b_r, 0)
     for k in range(1, plane):
         go(None, functools.partial(g_copy, k))
-    shard_go(at, a_s, a_r, 0)
-    go(upper, lambda: across(z))
     rg[:, h] = sg[h]
     for q in range(chunks):
         sx[q] = (
@@ -250,10 +263,12 @@
         for k in range(1, plane):
             go(None, functools.partial(x_copy, q, k))
         rx[q, :, h] = sx[q, h]
-    for k in range(1, lines):
-        shard_wait(bt, b_s, b_r, k)
-        if k < lines - 1:
-            shard_go(bt, b_s, b_r, k)
+        if q == 0:
+            b_step(1)
+            a_start(0)
+            a_start(1)
+    b_step(2)
+    b_step(3)
 
     cf[...] = jnp.zeros_like(cf)
     for k in range(1, plane):
@@ -267,7 +282,6 @@
         return copy(cf, c1, c_s, c_r, 0, own)
 
     go(upper, coef_copy)
-    a_step(1)
 
     def sums(value, cols, send_l, send_r, recv_l, recv_r, s_sem, r_sem):
         def left(t):
@@ -276,22 +290,21 @@
         def right(t):
             return copy(send_r.at[t], recv_r.at[t], s_sem.at[1, t], r_sem.at[1, t], seg, own + plane)
 
-        for t in range(lines - 1):
-            for goal, buf, got, make, cond, more in (
-                (t, send_l, recv_l, left, z > t, has_right),
-                (lines - 1 - t, send_r, recv_r, right, z < lines - 1 - t, has_left),
-            ):
-                @pl.when(cond & jnp.logical_not(more))
-                def _():
-                    buf[goal] = value(goal).astype(bf16)
-
-                @pl.when(cond & more)
-                def _():
-                    mine = value(goal)
-                    make(goal).wait_recv()
-                    buf[goal] = (mine + got[goal].astype(f32)).astype(bf16)
-
-                go(cond, functools.partial(make, goal))
+        def hop(stage):
+            for t in range(lines - 1 - stage):
+                for goal, buf, got, make, cond in (
+                    (t, send_l, recv_l, left, z == lines - 1 - stage),
+                    (lines - 1 - t, send_r, recv_r, right, z == stage),
+                ):
+                    @pl.when(cond)
+                    def _():
+                        mine = value(goal)
+                        if stage > 0:
+                            make(goal).wait_recv()
+                            mine += got[goal].astype(f32)
+                        buf[goal] = mine.astype(bf16)
+
+                    go(cond, functools.partial(make, goal))
 
         def finish(out):
             out[:, cols] = value(z)
@@ -306,78 +319,100 @@
                 right(z).wait_recv()
                 out[:, cols] += recv_r[z].astype(f32)
 
-        return finish
-
-    def down_sums(q):
-        for k in range(1, plane):
-            x_copy(q, k).wait_recv()
-        return sums(
-            lambda j: dot_nn(cft[j, :, :rows], rx[q, j].reshape(rows, part)),
+        return hop, finish
+
+    downs = [
+        sums(
+            lambda j, q=q: dot_nn(cft[j, :, :rows], rx[q, j].reshape(rows, part)),
             pl.ds(q * part, part),
             sl.at[q], sr.at[q], ql.at[q], qr.at[q], d_s.at[q], d_r.at[q],
         )
+        for q in range(chunks)
+    ]
+
+    def down_stage(m):
+        if m < chunks:
+            for k in range(1, plane):
+                x_copy(m, k).wait_recv()
+        for stage in range(lines - 1):
+            if 0 <= m - stage < chunks:
+                downs[m - stage][0](stage)
 
     order = (z, z + 1 - 2 * (z % 2), 2 - z // 2, 3 - 3 * (z // 2))
 
-    def t_copy(i, k):
+    def t_copy(p, i, k):
         return copy(
-            ts.at[order[i], (h + k) % plane], tr.at[h, order[i]],
-            t_s.at[i, k - 1], t_r.at[i, k - 1], seg, host(k),
-        )
-
-    def term(i):
+            ts.at[p, order[i], (h + k) % plane], tr.at[p, h, order[i]],
+            t_s.at[p, i, k - 1], t_r.at[p, i, k - 1], seg, host(k),
+        )
+
+    def term(i, p):
         j = order[i]
-        for q in range(chunks):
-            cols = pl.ds(q * part, part)
-            mine = dot_nn(cf[j, :, :rank_dim], at[j, :, cols]).astype(bf16)
-
-            @pl.when(upper)
-            def _():
-                ts[j, :, :, cols] = mine.reshape(plane, cap, part)
-
-            @pl.when(lower)
-            def _():
-                if q == 0:
-                    across(j).wait_recv()
-                above = dot_nn(c1[j, :, :rank_dim], a1[j, :, cols]).astype(bf16)
-                total = (mine.astype(f32) + above.astype(f32)).astype(bf16)
-                ts[j, :, :, cols] = total.reshape(plane, cap, part)
+        mine = dot_nn(cf[j, :, :rank_dim], at[p, j]).astype(bf16)
+
+        @pl.when(upper)
+        def _():
+            ts[p, j] = mine.reshape(plane, cap, wide)
+
+        @pl.when(lower)
+        def _():
+            across(p, j).wait_recv()
+            above = dot_nn(c1[j, :, :rank_dim], a1[p, j]).astype(bf16)
+            total = (mine.astype(f32) + above.astype(f32)).astype(bf16)
+            ts[p, j] = total.reshape(plane, cap, wide)
 
         for k in range(1, plane):
-            go(None, functools.partial(t_copy, i, k))
-        tr[h, j] = ts[j, h]
+            go(None, functools.partial(t_copy, p, i, k))
+        tr[p, h, j] = ts[p, j, h]
 
     def project(i):
         j = order[i]
         proj = jnp.zeros((rank_dim, rows), f32)
         for q in range(chunks):
-            proj += dot_nt(at[j, :, q * part : (q + 1) * part], rx[q, j].reshape(rows, part))
+            p, first = q * part // wide, q * part % wide
+            proj += dot_nt(at[p, j, :, first : first + part], rx[q, j].reshape(rows, part))
         gup[j] = dot_nn(proj.astype(bf16), rg[j].reshape(rows, out_width))
 
-    ends = [down_sums(0)]
+    up_hop, up_finish = sums(
+        lambda j: gup[j], pl.ds(0, out_width), ul, ur, vl, vr, u_s, u_r
+    )
+    down_stage(0)
+    a_step(1, 0)
+    down_stage(1)
+    a_step(1, 1)
+    down_stage(2)
+    a_step(2, 0)
+    down_stage(3)
+    a_step(2, 1)
     pl.when(lower)(lambda: coef_copy().wait_recv())
-    term(0)
-    a_step(2)
-    ends.append(down_sums(1))
-    term(1)
+    term(0, 0)
+    term(0, 1)
+    down_stage(4)
+    term(1, 0)
+    term(1, 1)
+    down_stage(5)
     project(0)
     project(1)
-    a_step(3)
-    term(2)
+    a_step(3, 0)
+    a_step(3, 1)
     project(2)
     project(3)
-    up_end = sums(lambda j: gup[j], pl.ds(0, out_width), ul, ur, vl, vr, u_s, u_r)
-    term(3)
-    for end in ends:
-        end(gd)
-    up_end(gu)
-    for i in range(lines):
-        for k in range(1, plane):
-            t_copy(i, k).wait_recv()
-    for q in range(chunks):
-        cols = pl.ds(q * part, part)
-        passed[:, cols] = dot_nn(
-            placing_t, tr[:, :, :, cols].reshape(plane * lines * cap, part)
+    up_hop(0)
+    term(2, 0)
+    term(2, 1)
+    up_hop(1)
+    term(3, 0)
+    up_hop(2)
+    term(3, 1)
+    for _, finish in downs:
+        finish(gd)
+    up_finish(gu)
+    for p in range(parts):
+        for i in range(lines):
+            for k in range(1, plane):
+                t_copy(p, i, k).wait_recv()
+        passed[:, p * wide : (p + 1) * wide] = dot_nn(
+            placing_t, tr[p].reshape(plane * lines * cap, wide)
         ).astype(bf16)
     for cond, make in pending:
         if cond is None:
@@ -401,6 +436,7 @@
     cap = 2 * tok // (lines * plane)
     rows = plane * cap
     part = width // chunks
+    wide = width // parts
     lanes = 128
     vmem = pl.BlockSpec(memory_space=pltpu.VMEM)
     dma = pltpu.SemaphoreType.DMA
@@ -418,14 +454,14 @@
             pltpu.VMEM((plane, lines, cap, out_width), bf16),
             pltpu.VMEM((chunks, lines, plane, cap, part), bf16),
             pltpu.VMEM((lines, plane, cap, out_width), bf16),
-            pltpu.VMEM((lines, rank_dim, width), bf16),
+            pltpu.VMEM((parts, lines, rank_dim, wide), bf16),
             pltpu.VMEM((lines, rank_dim, out_width), bf16),
-            pltpu.VMEM((lines, rank_dim, width), bf16),
+            pltpu.VMEM((parts, lines, rank_dim, wide), bf16),
             pltpu.VMEM((lines, rows, lanes), bf16),
             pltpu.VMEM((lines, rank_dim, lanes), bf16),
             pltpu.VMEM((lines, rows, lanes), bf16),
-            pltpu.VMEM((lines, plane, cap, width), bf16),
-            pltpu.VMEM((plane, lines, cap, width), bf16),
+            pltpu.VMEM((parts, lines, plane, cap, wide), bf16),
+            pltpu.VMEM((parts, plane, lines, cap, wide), bf16),
         ]
         + [pltpu.VMEM((chunks, lines, rank_dim, part), bf16)] * 4
         + [pltpu.VMEM((lines, rank_dim, out_width), bf16)] * 4
@@ -433,11 +469,11 @@
             pltpu.VMEM((lines, rank_dim, out_width), f32),
             dma((chunks, plane - 1)), dma((chunks, plane - 1)),
             dma((plane - 1,)), dma((plane - 1,)),
+            dma((parts, 2, lines)), dma((parts, lines)),
             dma((2, lines)), dma((lines,)),
-            dma((2, lines)), dma((lines,)),
-            dma((lines,)), dma((lines,)),
+            dma((parts, lines)), dma((parts, lines)),
             dma, dma,
-            dma((lines, plane - 1)), dma((lines, plane - 1)),
+            dma((parts, lines, plane - 1)), dma((parts, lines, plane - 1)),
             dma((chunks, 2, lines)), dma((chunks, 2, lines)),
             dma((2, lines)), dma((2, lines)),
         ],
@@ -449,7 +485,7 @@
         x,
         g,
         tenant.reshape(1, tok),
-        adapter_owner_index.reshape(-1, 1),
+        adapter_owner_index.reshape(1, -1),
         adapter_down_weight[0, 0].T,
         adapter_up_weight[0, 0],
     )

time: 93.4 us -> 87.3 us (0.935)
  the two profiles are of different devices: /device:TPU:17 before, /device:TPU:0 now
where the time goes in v2:
time: 87.3 us; the launch traced here: 87.1 us
  Pallas kernels  82.3 us (94%)
  local copies, waits for them, and re-layouts  4.17 us (5%)
    pallas_call x1, Pallas kernels, local_lines(): pl.pallas_call(lines_kernel, out_shape=(jax.ShapeDtypeStruct((tok, width)...  82.3 us
    unnamed x7, local copies, waits for them, and re-layouts  4.17 us

profile of v2, /device:TPU:0, one launch (start us, length us, event | category | flops | bytes accessed | tf_op | source)
XLA Modules:
  0.0 87.1 jit_solution(11116570007453583711)
XLA Ops:
  0.6 82.3 %adapter_lines.1 = (bf16[128,4096]{1,0:T(8,128)(2,1)}, f32[64,4096]{1,0:T(8,128)}, f32[64,1024]{1,0:T(8,128)}) custom-call(bf16[128,4096]{1,0:T(8,128)(2,1)} %bitcast.13, bf16[128,1024]{1,0:T(8,128)(2,1)} %bitcast.17, s32[1,128]{1,0:T(1,128)} %bitcast.20, s32[1,16]{1,0:T(1,128)} %bitcast.21, bf16[64,4096]{1,0:T(8,128)(2,1)} %bitcast.16, ...), custom_call_target="tpu_custom_call" | custom-call | tf_op jit(solution)/shard_map/adapter_lines/pallas_call | solution.py:443
  82.9 0.0 copy-start
  82.9 2.4 %copy.12 = bf16[1,128,4096]{2,1,0:T(8,128)(2,1)} copy(bf16[1,128,4096]{2,1,0:T(8,128)(2,1)} %bitcast.15) | data formatting | bytes 2097152
  85.3 0.0 copy-done
  85.3 0.0 copy-start.1
  85.3 1.0 %copy.13 = f32[1,1,4096,64]{2,3,1,0:T(8,128)} copy(f32[1,1,4096,64]{2,3,1,0:T(8,128)S(1)} %bitcast.14) | data formatting | bytes 2097152
  86.3 0.1 copy-done.1
  86.4 0.7 copy.14
Async XLA Ops:
  82.9 2.4 %copy-start = (f32[64,4096]{1,0:T(8,128)S(1)}, f32[64,4096]{1,0:T(8,128)}, u32[]{:S(2)}) copy-start(f32[64,4096]{1,0:T(8,128)} %get-tuple-element.7) | copy-start | bytes 3145732
  85.3 1.1 %copy-start.1 = (f32[64,1024]{1,0:T(8,128)S(1)}, f32[64,1024]{1,0:T(8,128)}, u32[]{:S(2)}) copy-start(f32[64,1024]{1,0:T(8,128)} %get-tuple-element.8) | copy-start | bytes 786436

commit v3 on v2

--- a/solution.py
+++ b/solution.py
@@ -125,7 +125,7 @@
 def lines_kernel(
     x, g, ids, owner_of, a, b,
     passed, gd, gu,
-    sx, sg, rx, rg, at, bt, a1, cf, cft, c1, ts, tr, sl, sr, ql, qr, ul, ur, vl, vr, gup,
+    sx, sg, rx, rg, at, bt, cf, cft, c1, ts, tr, sl, sr, ql, qr, ul, ur, vl, vr, gup,
     x_s, x_r, g_s, g_r, a_s, a_r, b_s, b_r, a1_s, a1_r, c_s, c_r, t_s, t_r, d_s, d_r, u_s, u_r,
 ):
     tok, width = x.shape
@@ -197,48 +197,55 @@
 
     bt[z] = b[...]
     for p in range(parts):
-        at[p, z] = a[:, p * wide : (p + 1) * wide]
+        at[p, z, :rank_dim] = a[:, p * wide : (p + 1) * wide]
     sg[...] = dot_nn(placing, g[...]).astype(bf16).reshape(plane, lines, cap, out_width)
     pl.semaphore_wait(
         barrier, plane + jnp.where(has_left, 1, 0) + jnp.where(has_right, 1, 0)
     )
 
-    def shard_go(buf, send, recv, k):
-        go(
-            (z >= k) & has_right,
-            lambda: copy(buf.at[z - k], buf.at[z - k], send.at[0, k], recv.at[z - k], seg, own + plane),
-        )
-        go(
-            (z + k < lines) & has_left,
-            lambda: copy(buf.at[z + k], buf.at[z + k], send.at[1, k], recv.at[z + k], seg, own - plane),
-        )
-
-    def shard_wait(buf, send, recv, k):
-        pl.when(z >= k)(
-            lambda: copy(buf.at[z - k], buf.at[z - k], send.at[0, k], recv.at[z - k], seg, host(1)).wait_recv()
-        )
-        pl.when(z + k < lines)(
-            lambda: copy(buf.at[z + k], buf.at[z + k], send.at[1, k], recv.at[z + k], seg, host(1)).wait_recv()
-        )
+    def shard_right(view, send, recv, k):
+        ref = view(z - k)
+        return copy(ref, ref, send.at[0, k], recv.at[z - k], seg, own + plane)
+
+    def shard_left(view, send, recv, k):
+        ref = view(z + k)
+        return copy(ref, ref, send.at[1, k], recv.at[z + k], seg, own - plane)
+
+    def shard_go(view, send, recv, k):
+        go((z >= k) & has_right, lambda: shard_right(view, send, recv, k))
+        go((z + k < lines) & has_left, lambda: shard_left(view, send, recv, k))
+
+    def shard_wait(view, send, recv, k):
+        pl.when(z >= k)(lambda: shard_right(view, send, recv, k).wait_recv())
+        pl.when(z + k < lines)(lambda: shard_left(view, send, recv, k).wait_recv())
+
+    def b_view(j):
+        return bt.at[j]
+
+    def a_view(p):
+        return lambda j: at.at[p, j, pl.ds(0, rank_dim)]
 
     def across(p, j):
-        return copy(at.at[p, j], a1.at[p, j], a1_s.at[p, j], a1_r.at[p, j], 0, own)
+        return copy(
+            at.at[p, j, pl.ds(0, rank_dim)], at.at[p, j, pl.ds(rank_dim, rank_dim)],
+            a1_s.at[p, j], a1_r.at[p, j], 0, own,
+        )
 
     def a_start(p):
-        shard_go(at.at[p], a_s.at[p], a_r.at[p], 0)
+        shard_go(a_view(p), a_s.at[p], a_r.at[p], 0)
         go(upper, lambda: across(p, z))
 
     def a_step(k, p):
-        shard_wait(at.at[p], a_s.at[p], a_r.at[p], k)
+        shard_wait(a_view(p), a_s.at[p], a_r.at[p], k)
         if k < lines - 1:
-            shard_go(at.at[p], a_s.at[p], a_r.at[p], k)
+            shard_go(a_view(p), a_s.at[p], a_r.at[p], k)
         go((z >= k) & upper, lambda: across(p, z - k))
         go((z + k < lines) & upper, lambda: across(p, z + k))
 
     def b_step(k):
-        shard_wait(bt, b_s, b_r, k)
+        shard_wait(b_view, b_s, b_r, k)
         if k < lines - 1:
-            shard_go(bt, b_s, b_r, k)
+            shard_go(b_view, b_s, b_r, k)
 
     def g_copy(k):
         return copy(
@@ -250,7 +257,7 @@
             sx.at[q, (h + k) % plane], rx.at[q, :, h], x_s.at[q, k - 1], x_r.at[q, k - 1], seg, host(k)
         )
 
-    shard_go(bt, b_s, b_r, 0)
+    shard_go(b_view, b_s, b_r, 0)
     for k in range(1, plane):
         go(None, functools.partial(g_copy, k))
     rg[:, h] = sg[h]
@@ -265,23 +272,20 @@
         rx[q, :, h] = sx[q, h]
         if q == 0:
             b_step(1)
+        if q == 1:
+            b_step(2)
             a_start(0)
             a_start(1)
-    b_step(2)
     b_step(3)
 
-    cf[...] = jnp.zeros_like(cf)
     for k in range(1, plane):
         g_copy(k).wait_recv()
     for j in range(lines):
         grads = rg[j].reshape(rows, out_width)
-        cf[j, :, :rank_dim] = (adapter_scale * dot_nt(grads, bt[j])).astype(bf16)
         cft[j, :, :rows] = (adapter_scale * dot_nt(bt[j], grads)).astype(bf16)
 
     def coef_copy():
         return copy(cf, c1, c_s, c_r, 0, own)
-
-    go(upper, coef_copy)
 
     def sums(value, cols, send_l, send_r, recv_l, recv_r, s_sem, r_sem):
         def left(t):
@@ -348,18 +352,17 @@
 
     def term(i, p):
         j = order[i]
-        mine = dot_nn(cf[j, :, :rank_dim], at[p, j]).astype(bf16)
 
         @pl.when(upper)
         def _():
-            ts[p, j] = mine.reshape(plane, cap, wide)
+            total = dot_nn(cf[j, :, :rank_dim], at[p, j, :rank_dim])
+            ts[p, j] = total.astype(bf16).reshape(plane, cap, wide)
 
         @pl.when(lower)
         def _():
             across(p, j).wait_recv()
-            above = dot_nn(c1[j, :, :rank_dim], a1[p, j]).astype(bf16)
-            total = (mine.astype(f32) + above.astype(f32)).astype(bf16)
-            ts[p, j] = total.reshape(plane, cap, wide)
+            total = dot_nn(cf[j, :, : 2 * rank_dim], at[p, j])
+            ts[p, j] = total.astype(bf16).reshape(plane, cap, wide)
 
         for k in range(1, plane):
             go(None, functools.partial(t_copy, p, i, k))
@@ -370,13 +373,18 @@
         proj = jnp.zeros((rank_dim, rows), f32)
         for q in range(chunks):
             p, first = q * part // wide, q * part % wide
-            proj += dot_nt(at[p, j, :, first : first + part], rx[q, j].reshape(rows, part))
+            proj += dot_nt(at[p, j, :rank_dim, first : first + part], rx[q, j].reshape(rows, part))
         gup[j] = dot_nn(proj.astype(bf16), rg[j].reshape(rows, out_width))
 
     up_hop, up_finish = sums(
         lambda j: gup[j], pl.ds(0, out_width), ul, ur, vl, vr, u_s, u_r
     )
     down_stage(0)
+    cf[...] = jnp.zeros_like(cf)
+    for j in range(lines):
+        grads = rg[j].reshape(rows, out_width)
+        cf[j, :, :rank_dim] = (adapter_scale * dot_nt(grads, bt[j])).astype(bf16)
+    go(upper, coef_copy)
     a_step(1, 0)
     down_stage(1)
     a_step(1, 1)
@@ -384,7 +392,12 @@
     a_step(2, 0)
     down_stage(3)
     a_step(2, 1)
-    pl.when(lower)(lambda: coef_copy().wait_recv())
+
+    @pl.when(lower)
+    def _():
+        coef_copy().wait_recv()
+        cf[:, :, rank_dim : 2 * rank_dim] = c1[:, :, :rank_dim]
+
     term(0, 0)
     term(0, 1)
     down_stage(4)
@@ -454,9 +467,8 @@
             pltpu.VMEM((plane, lines, cap, out_width), bf16),
             pltpu.VMEM((chunks, lines, plane, cap, part), bf16),
             pltpu.VMEM((lines, plane, cap, out_width), bf16),
-            pltpu.VMEM((parts, lines, rank_dim, wide), bf16),
+            pltpu.VMEM((parts, lines, 2 * rank_dim, wide), bf16),
             pltpu.VMEM((lines, rank_dim, out_width), bf16),
-            pltpu.VMEM((parts, lines, rank_dim, wide), bf16),
             pltpu.VMEM((lines, rows, lanes), bf16),
             pltpu.VMEM((lines, rank_dim, lanes), bf16),
             pltpu.VMEM((lines, rows, lanes), bf16),

time: 87.3 us -> 83 us (0.951)
  Pallas kernels: 82.3 us -> 78 us
    pallas_call x1, Pallas kernels: 82.3 us -> 78 us  [local_lines(): pl.pallas_call(lines_kernel, out_shape=(jax.ShapeDtypeStruct((tok, width)...]
where the time goes in v3:
time: 83 us; the launch traced here: 82.8 us
  Pallas kernels  78 us (94%)
  local copies, waits for them, and re-layouts  4.17 us (5%)
    pallas_call x1, Pallas kernels, local_lines(): pl.pallas_call(lines_kernel, out_shape=(jax.ShapeDtypeStruct((tok, width)...  78 us
    unnamed x7, local copies, waits for them, and re-layouts  4.17 us

profile of v3, /device:TPU:0, one launch (start us, length us, event | category | flops | bytes accessed | tf_op | source)
XLA Modules:
  0.0 82.8 jit_solution(8671770325183077022)
XLA Ops:
  0.6 78.0 %adapter_lines.1 = (bf16[128,4096]{1,0:T(8,128)(2,1)}, f32[64,4096]{1,0:T(8,128)}, f32[64,1024]{1,0:T(8,128)}) custom-call(bf16[128,4096]{1,0:T(8,128)(2,1)} %bitcast.13, bf16[128,1024]{1,0:T(8,128)(2,1)} %bitcast.17, s32[1,128]{1,0:T(1,128)} %bitcast.20, s32[1,16]{1,0:T(1,128)} %bitcast.21, bf16[64,4096]{1,0:T(8,128)(2,1)} %bitcast.16, ...), custom_call_target="tpu_custom_call" | custom-call | tf_op jit(solution)/shard_map/adapter_lines/pallas_call | solution.py:456
  78.7 0.0 copy-start
  78.7 2.4 %copy.12 = bf16[1,128,4096]{2,1,0:T(8,128)(2,1)} copy(bf16[1,128,4096]{2,1,0:T(8,128)(2,1)} %bitcast.15) | data formatting | bytes 2097152
  81.0 0.0 copy-done
  81.0 0.0 copy-start.1
  81.0 1.0 %copy.13 = f32[1,1,4096,64]{2,3,1,0:T(8,128)} copy(f32[1,1,4096,64]{2,3,1,0:T(8,128)S(1)} %bitcast.14) | data formatting | bytes 2097152
  82.0 0.1 copy-done.1
  82.1 0.7 copy.14
Async XLA Ops:
  78.7 2.4 %copy-start = (f32[64,4096]{1,0:T(8,128)S(1)}, f32[64,4096]{1,0:T(8,128)}, u32[]{:S(2)}) copy-start(f32[64,4096]{1,0:T(8,128)} %get-tuple-element.7) | copy-start | bytes 3145732
  81.0 1.1 %copy-start.1 = (f32[64,1024]{1,0:T(8,128)S(1)}, f32[64,1024]{1,0:T(8,128)}, u32[]{:S(2)}) copy-start(f32[64,1024]{1,0:T(8,128)} %get-tuple-element.8) | copy-start | bytes 786436

commit v4 on v3

--- a/solution.py
+++ b/solution.py
@@ -233,7 +233,6 @@
 
     def a_start(p):
         shard_go(a_view(p), a_s.at[p], a_r.at[p], 0)
-        go(upper, lambda: across(p, z))
 
     def a_step(k, p):
         shard_wait(a_view(p), a_s.at[p], a_r.at[p], k)
@@ -258,6 +257,8 @@
         )
 
     shard_go(b_view, b_s, b_r, 0)
+    for p in range(parts):
+        go(upper, functools.partial(across, p, z))
     for k in range(1, plane):
         go(None, functools.partial(g_copy, k))
     rg[:, h] = sg[h]
@@ -335,9 +336,9 @@
     ]
 
     def down_stage(m):
-        if m < chunks:
+        for q in {chunks - 2: (chunks - 2, chunks - 1)}.get(m, (m,) if m < chunks - 2 else ()):
             for k in range(1, plane):
-                x_copy(m, k).wait_recv()
+                x_copy(q, k).wait_recv()
         for stage in range(lines - 1):
             if 0 <= m - stage < chunks:
                 downs[m - stage][0](stage)
@@ -386,11 +387,9 @@
         cf[j, :, :rank_dim] = (adapter_scale * dot_nt(grads, bt[j])).astype(bf16)
     go(upper, coef_copy)
     a_step(1, 0)
+    a_step(1, 1)
     down_stage(1)
-    a_step(1, 1)
-    down_stage(2)
     a_step(2, 0)
-    down_stage(3)
     a_step(2, 1)
 
     @pl.when(lower)
@@ -400,23 +399,25 @@
 
     term(0, 0)
     term(0, 1)
-    down_stage(4)
-    term(1, 0)
-    term(1, 1)
-    down_stage(5)
+    down_stage(2)
     project(0)
     project(1)
     a_step(3, 0)
     a_step(3, 1)
+    term(1, 0)
+    term(1, 1)
+    down_stage(3)
     project(2)
     project(3)
     up_hop(0)
     term(2, 0)
     term(2, 1)
+    down_stage(4)
+    term(3, 0)
     up_hop(1)
-    term(3, 0)
+    down_stage(5)
+    term(3, 1)
     up_hop(2)
-    term(3, 1)
     for _, finish in downs:
         finish(gd)
     up_finish(gu)

time: 83 us -> 84.1 us (1.013)
  Pallas kernels: 78 us -> 79 us
    pallas_call x1, Pallas kernels: 78 us -> 79 us  [local_lines(): pl.pallas_call(lines_kernel, out_shape=(jax.ShapeDtypeStruct((tok, width)...]
where the time goes in v4:
time: 84.1 us; the launch traced here: 83.9 us
  Pallas kernels  79 us (94%)
  local copies, waits for them, and re-layouts  4.17 us (5%)
    pallas_call x1, Pallas kernels, local_lines(): pl.pallas_call(lines_kernel, out_shape=(jax.ShapeDtypeStruct((tok, width)...  79 us
    unnamed x7, local copies, waits for them, and re-layouts  4.17 us

profile of v4, /device:TPU:0, one launch (start us, length us, event | category | flops | bytes accessed | tf_op | source)
XLA Modules:
  0.0 83.9 jit_solution(7236962681435637142)
XLA Ops:
  0.6 79.0 %adapter_lines.1 = (bf16[128,4096]{1,0:T(8,128)(2,1)}, f32[64,4096]{1,0:T(8,128)}, f32[64,1024]{1,0:T(8,128)}) custom-call(bf16[128,4096]{1,0:T(8,128)(2,1)} %bitcast.13, bf16[128,1024]{1,0:T(8,128)(2,1)} %bitcast.17, s32[1,128]{1,0:T(1,128)} %bitcast.20, s32[1,16]{1,0:T(1,128)} %bitcast.21, bf16[64,4096]{1,0:T(8,128)(2,1)} %bitcast.16, ...), custom_call_target="tpu_custom_call" | custom-call | tf_op jit(solution)/shard_map/adapter_lines/pallas_call | solution.py:457
  79.7 0.0 copy-start
  79.7 2.4 %copy.12 = bf16[1,128,4096]{2,1,0:T(8,128)(2,1)} copy(bf16[1,128,4096]{2,1,0:T(8,128)(2,1)} %bitcast.15) | data formatting | bytes 2097152
  82.1 0.0 copy-done
  82.1 0.0 copy-start.1
  82.1 1.0 %copy.13 = f32[1,1,4096,64]{2,3,1,0:T(8,128)} copy(f32[1,1,4096,64]{2,3,1,0:T(8,128)S(1)} %bitcast.14) | data formatting | bytes 2097152
  83.0 0.1 copy-done.1
  83.2 0.7 copy.14
Async XLA Ops:
  79.7 2.4 %copy-start = (f32[64,4096]{1,0:T(8,128)S(1)}, f32[64,4096]{1,0:T(8,128)}, u32[]{:S(2)}) copy-start(f32[64,4096]{1,0:T(8,128)} %get-tuple-element.7) | copy-start | bytes 3145732
  82.1 1.1 %copy-start.1 = (f32[64,1024]{1,0:T(8,128)S(1)}, f32[64,1024]{1,0:T(8,128)}, u32[]{:S(2)}) copy-start(f32[64,1024]{1,0:T(8,128)} %get-tuple-element.8) | copy-start | bytes 786436

commit v5 on v4

--- a/solution.py
+++ b/solution.py
@@ -124,9 +124,9 @@
 
 def lines_kernel(
     x, g, ids, owner_of, a, b,
-    passed, gd, gu,
+    returned, back, gd, gu,
     sx, sg, rx, rg, at, bt, cf, cft, c1, ts, tr, sl, sr, ql, qr, ul, ur, vl, vr, gup,
-    x_s, x_r, g_s, g_r, a_s, a_r, b_s, b_r, a1_s, a1_r, c_s, c_r, t_s, t_r, d_s, d_r, u_s, u_r,
+    x_s, x_r, g_s, g_r, a_s, a_r, b_s, b_r, a1_s, a1_r, c_s, c_r, t_s, t_r, d_s, d_r, u_s, u_r, o_s,
 ):
     tok, width = x.shape
     out_width = g.shape[1]
@@ -193,7 +193,7 @@
         lax.broadcasted_iota(jnp.int32, (plane * lines * cap, tok), 0) == target
     ).astype(f32)
     placing = placing32.astype(bf16)
-    placing_t = placing32.T.astype(bf16)
+    back[...] = placing32.T.astype(bf16)
 
     bt[z] = b[...]
     for p in range(parts):
@@ -335,13 +335,11 @@
         for q in range(chunks)
     ]
 
-    def down_stage(m):
-        for q in {chunks - 2: (chunks - 2, chunks - 1)}.get(m, (m,) if m < chunks - 2 else ()):
+    def down_hop(q, stage):
+        if stage == 0:
             for k in range(1, plane):
                 x_copy(q, k).wait_recv()
-        for stage in range(lines - 1):
-            if 0 <= m - stage < chunks:
-                downs[m - stage][0](stage)
+        downs[q][0](stage)
 
     order = (z, z + 1 - 2 * (z % 2), 2 - z // 2, 3 - 3 * (z // 2))
 
@@ -380,16 +378,19 @@
     up_hop, up_finish = sums(
         lambda j: gup[j], pl.ds(0, out_width), ul, ur, vl, vr, u_s, u_r
     )
-    down_stage(0)
+    down_hop(0, 0)
     cf[...] = jnp.zeros_like(cf)
     for j in range(lines):
         grads = rg[j].reshape(rows, out_width)
         cf[j, :, :rank_dim] = (adapter_scale * dot_nt(grads, bt[j])).astype(bf16)
     go(upper, coef_copy)
+    down_hop(1, 0)
     a_step(1, 0)
     a_step(1, 1)
-    down_stage(1)
+    down_hop(2, 0)
+    down_hop(0, 1)
     a_step(2, 0)
+    down_hop(3, 0)
     a_step(2, 1)
 
     @pl.when(lower)
@@ -399,23 +400,26 @@
 
     term(0, 0)
     term(0, 1)
-    down_stage(2)
+    down_hop(1, 1)
+    down_hop(0, 2)
+    term(1, 0)
+    term(1, 1)
+    down_hop(2, 1)
+    down_hop(1, 2)
+    term(2, 0)
+    term(2, 1)
     project(0)
     project(1)
     a_step(3, 0)
     a_step(3, 1)
-    term(1, 0)
-    term(1, 1)
-    down_stage(3)
     project(2)
     project(3)
     up_hop(0)
-    term(2, 0)
-    term(2, 1)
-    down_stage(4)
+    down_hop(3, 1)
+    down_hop(2, 2)
     term(3, 0)
     up_hop(1)
-    down_stage(5)
+    down_hop(3, 2)
     term(3, 1)
     up_hop(2)
     for _, finish in downs:
@@ -425,14 +429,20 @@
         for i in range(lines):
             for k in range(1, plane):
                 t_copy(p, i, k).wait_recv()
-        passed[:, p * wide : (p + 1) * wide] = dot_nn(
-            placing_t, tr[p].reshape(plane * lines * cap, wide)
-        ).astype(bf16)
+        pltpu.make_async_copy(tr.at[p], returned.at[p], o_s.at[p]).start()
+    for p in range(parts):
+        pltpu.make_async_copy(tr.at[p], returned.at[p], o_s.at[p]).wait()
     for cond, make in pending:
         if cond is None:
             make().wait_send()
         else:
             pl.when(cond)(functools.partial(lambda make: make().wait_send(), make))
+
+
+def select_kernel(returned, back, gd_in, gu_in, passed, gd, gu):
+    passed[...] = dot_nn(back[...], returned[0]).astype(bf16)
+    gd[...] = gd_in[...]
+    gu[...] = gu_in[...]
 
 
 def local_lines(
@@ -451,18 +461,20 @@
     rows = plane * cap
     part = width // chunks
     wide = width // parts
+    slots = plane * lines * cap
     lanes = 128
     vmem = pl.BlockSpec(memory_space=pltpu.VMEM)
     dma = pltpu.SemaphoreType.DMA
-    passed, gd, gu = pl.pallas_call(
+    returned, back, gd, gu = pl.pallas_call(
         lines_kernel,
         out_shape=(
-            jax.ShapeDtypeStruct((tok, width), bf16),
+            jax.ShapeDtypeStruct((parts, plane, lines, cap, wide), bf16),
+            jax.ShapeDtypeStruct((tok, slots), bf16),
             jax.ShapeDtypeStruct((rank_dim, width), f32),
             jax.ShapeDtypeStruct((rank_dim, out_width), f32),
         ),
         in_specs=[vmem] * 6,
-        out_specs=(vmem,) * 3,
+        out_specs=(pl.BlockSpec(memory_space=pl.ANY),) + (vmem,) * 3,
         scratch_shapes=[
             pltpu.VMEM((chunks, plane, lines, cap, part), bf16),
             pltpu.VMEM((plane, lines, cap, out_width), bf16),
@@ -489,6 +501,7 @@
             dma((parts, lines, plane - 1)), dma((parts, lines, plane - 1)),
             dma((chunks, 2, lines)), dma((chunks, 2, lines)),
             dma((2, lines)), dma((2, lines)),
+            dma((parts,)),
         ],
         compiler_params=pltpu.CompilerParams(
             collective_id=0, has_side_effects=True, vmem_limit_bytes=56 * 1024 * 1024
@@ -502,6 +515,29 @@
         adapter_down_weight[0, 0].T,
         adapter_up_weight[0, 0],
     )
+    tiles = 4
+    tile, each = width // tiles, tiles // parts
+    columns = lambda c: (0, c)
+    down_spec = pl.BlockSpec((rank_dim, tile), columns)
+    up_spec = pl.BlockSpec((rank_dim, out_width // tiles), columns)
+    passed, gd, gu = pl.pallas_call(
+        select_kernel,
+        grid=(tiles,),
+        out_shape=(
+            jax.ShapeDtypeStruct((tok, width), bf16),
+            jax.ShapeDtypeStruct((rank_dim, width), f32),
+            jax.ShapeDtypeStruct((rank_dim, out_width), f32),
+        ),
+        in_specs=[
+            pl.BlockSpec((1, slots, tile), lambda c: (c // each, 0, c % each)),
+            pl.BlockSpec((tok, slots), lambda c: (0, 0)),
+            down_spec,
+            up_spec,
+        ],
+        out_specs=(pl.BlockSpec((tok, tile), columns), down_spec, up_spec),
+        compiler_params=pltpu.CompilerParams(vmem_limit_bytes=56 * 1024 * 1024),
+        name="select_rows",
+    )(returned.reshape(parts, slots, wide), back, gd, gu)
     return (passed[None], gd.T[None, None], gu[None, None])
 
 

time: 84.1 us -> 83.5 us (level)
  local copies, waits for them, and re-layouts: 4.17 us -> 0 us
  Pallas kernels: 79 us -> 82.7 us
    unnamed x7 -> x0, local copies, waits for them, and re-layouts: 4.17 us -> none
    pallas_call x1 -> x2, Pallas kernels: 79 us -> 82.7 us  [the longest x1 78.4 us: local_lines(): pl.pallas_call(lines_kernel, out_shape=(jax.ShapeDtypeStruct((parts, plan...]
where the time goes in v5:
time: 83.5 us; the launch traced here: 83.3 us
  Pallas kernels  82.7 us (99%)
    pallas_call x1, Pallas kernels, local_lines(): pl.pallas_call(lines_kernel, out_shape=(jax.ShapeDtypeStruct((parts, plan...  78.4 us
    pallas_call x1, Pallas kernels, local_lines(): pl.pallas_call(select_kernel, grid=(tiles,), out_shape=(jax.ShapeDtypeStr...  4.32 us

profile of v5, /device:TPU:0, one launch (start us, length us, event | category | flops | bytes accessed | tf_op | source)
XLA Modules:
  0.0 83.3 jit_solution(9316648016164037072)
XLA Ops:
  0.6 78.4 %adapter_lines.1 = (bf16[2,4,4,16,2048]{4,3,2,1,0:T(8,128)(2,1)}, bf16[128,256]{1,0:T(8,128)(2,1)}, f32[64,4096]{1,0:T(8,128)}, f32[64,1024]{1,0:T(8,128)}) custom-call(bf16[128,4096]{1,0:T(8,128)(2,1)} %bitcast.15, bf16[128,1024]{1,0:T(8,128)(2,1)} %bitcast.17, s32[1,128]{1,0:T(1,128)} %bitcast.19, s32[1,16]{1,0:T(1,128)} %bitcast.20, ...), custom_call_target="tpu_custom_call" | custom-call | tf_op jit(solution)/shard_map/adapter_lines/pallas_call | solution.py:468
  79.0 4.3 %select_rows.1 = (bf16[128,4096]{1,0:T(8,128)(2,1)}, f32[64,4096]{1,0:T(8,128)}, f32[64,1024]{1,0:T(8,128)}) custom-call(bf16[2,256,2048]{2,1,0:T(8,128)(2,1)} %bitcast.14, bf16[128,256]{1,0:T(8,128)(2,1)} %get-tuple-element.11.back, f32[64,4096]{1,0:T(8,128)} %get-tuple-element.12.gd_in, f32[64,1024]{1,0:T(8,128)} %get-tuple-element.13.gu_in), custom_call_target="tpu_custom_call" | custom-call | tf_op jit(solution)/shard_map/select_rows/pallas_call | solution.py:523

commit v6 on v5

--- a/solution.py
+++ b/solution.py
@@ -125,8 +125,8 @@
 def lines_kernel(
     x, g, ids, owner_of, a, b,
     returned, back, gd, gu,
-    sx, sg, rx, rg, at, bt, cf, cft, c1, ts, tr, sl, sr, ql, qr, ul, ur, vl, vr, gup,
-    x_s, x_r, g_s, g_r, a_s, a_r, b_s, b_r, a1_s, a1_r, c_s, c_r, t_s, t_r, d_s, d_r, u_s, u_r, o_s,
+    sx, sg, rx, rg, at, cfo, cfto, cf, cft, c1, ts, tr, sl, sr, ql, qr, pjs, pjr,
+    x_s, x_r, g_s, g_r, a_s, a_r, a1_s, a1_r, c_s, c_r, t_s, t_r, d_s, d_r, f_s, f_r, p_s, p_r, o_s,
 ):
     tok, width = x.shape
     out_width = g.shape[1]
@@ -168,11 +168,9 @@
     has_right = z < lines - 1
 
     barrier = pltpu.get_barrier_semaphore()
-    for k in range(1, plane):
-        signal(seg, host(k))
+    for k in range(1, lines * plane):
+        signal(seg, (own + k) % (lines * plane))
     signal(1 - seg, own)
-    pl.when(has_left)(lambda: signal(seg, own - plane))
-    pl.when(has_right)(lambda: signal(seg, own + plane))
 
     n_owner = lines * plane
     n_adapter = owner_of.shape[1]
@@ -195,13 +193,10 @@
     placing = placing32.astype(bf16)
     back[...] = placing32.T.astype(bf16)
 
-    bt[z] = b[...]
     for p in range(parts):
         at[p, z, :rank_dim] = a[:, p * wide : (p + 1) * wide]
     sg[...] = dot_nn(placing, g[...]).astype(bf16).reshape(plane, lines, cap, out_width)
-    pl.semaphore_wait(
-        barrier, plane + jnp.where(has_left, 1, 0) + jnp.where(has_right, 1, 0)
-    )
+    pl.semaphore_wait(barrier, lines * plane)
 
     def shard_right(view, send, recv, k):
         ref = view(z - k)
@@ -218,9 +213,6 @@
     def shard_wait(view, send, recv, k):
         pl.when(z >= k)(lambda: shard_right(view, send, recv, k).wait_recv())
         pl.when(z + k < lines)(lambda: shard_left(view, send, recv, k).wait_recv())
-
-    def b_view(j):
-        return bt.at[j]
 
     def a_view(p):
         return lambda j: at.at[p, j, pl.ds(0, rank_dim)]
@@ -241,14 +233,12 @@
         go((z >= k) & upper, lambda: across(p, z - k))
         go((z + k < lines) & upper, lambda: across(p, z + k))
 
-    def b_step(k):
-        shard_wait(b_view, b_s, b_r, k)
-        if k < lines - 1:
-            shard_go(b_view, b_s, b_r, k)
-
-    def g_copy(k):
+    pairs = [(d, k) for d in range(lines) for k in range(plane) if d + k > 0]
+
+    def g_copy(d, k):
+        goal, place = (z + d) % lines, (h + k) % plane
         return copy(
-            sg.at[(h + k) % plane], rg.at[:, h], g_s.at[k - 1], g_r.at[k - 1], seg, host(k)
+            sg.at[place, goal], rg.at[z, h], g_s.at[d, k], g_r.at[d, k], seg, goal * plane + place
         )
 
     def x_copy(q, k):
@@ -256,12 +246,11 @@
             sx.at[q, (h + k) % plane], rx.at[q, :, h], x_s.at[q, k - 1], x_r.at[q, k - 1], seg, host(k)
         )
 
-    shard_go(b_view, b_s, b_r, 0)
+    for d, k in pairs:
+        go(None, functools.partial(g_copy, d, k))
+    rg[z, h] = sg[h, z]
     for p in range(parts):
         go(upper, functools.partial(across, p, z))
-    for k in range(1, plane):
-        go(None, functools.partial(g_copy, k))
-    rg[:, h] = sg[h]
     for q in range(chunks):
         sx[q] = (
             dot_nn(placing, x[:, q * part : (q + 1) * part])
@@ -271,19 +260,33 @@
         for k in range(1, plane):
             go(None, functools.partial(x_copy, q, k))
         rx[q, :, h] = sx[q, h]
-        if q == 0:
-            b_step(1)
-        if q == 1:
-            b_step(2)
-            a_start(0)
-            a_start(1)
-    b_step(3)
-
-    for k in range(1, plane):
-        g_copy(k).wait_recv()
+    a_start(0)
+
+    cfo[...] = jnp.zeros_like(cfo)
+    cfto[...] = jnp.zeros_like(cfto)
+    pjs[...] = jnp.zeros_like(pjs)
+    for d, k in pairs:
+        g_copy(d, k).wait_recv()
     for j in range(lines):
         grads = rg[j].reshape(rows, out_width)
-        cft[j, :, :rows] = (adapter_scale * dot_nt(bt[j], grads)).astype(bf16)
+        cfto[j, :, :rows] = (adapter_scale * dot_nt(b[...], grads)).astype(bf16)
+        cfo[j, :, :rank_dim] = (adapter_scale * dot_nt(grads, b[...])).astype(bf16)
+
+    def coef_back(d, which):
+        goal = (z + d) % lines
+        source, sink = ((cfto, cft), (cfo, cf))[which]
+        return copy(
+            source.at[goal], sink.at[z], f_s.at[which, d], f_r.at[which, d], seg, goal * plane + h
+        )
+
+    for which in range(2):
+        for d in range(1, lines):
+            go(None, functools.partial(coef_back, d, which))
+    cft[z] = cfto[z]
+    cf[z] = cfo[z]
+    a_start(1)
+    for d in range(1, lines):
+        coef_back(d, 0).wait_recv()
 
     def coef_copy():
         return copy(cf, c1, c_s, c_r, 0, own)
@@ -373,16 +376,15 @@
         for q in range(chunks):
             p, first = q * part // wide, q * part % wide
             proj += dot_nt(at[p, j, :rank_dim, first : first + part], rx[q, j].reshape(rows, part))
-        gup[j] = dot_nn(proj.astype(bf16), rg[j].reshape(rows, out_width))
-
-    up_hop, up_finish = sums(
-        lambda j: gup[j], pl.ds(0, out_width), ul, ur, vl, vr, u_s, u_r
-    )
+        if i == 0:
+            pjr[z, :, :rows] = proj.astype(bf16)
+        else:
+            pjs[j, :, :rows] = proj.astype(bf16)
+            go(None, lambda: copy(pjs.at[j], pjr.at[z], p_s.at[i], p_r.at[z], seg, j * plane + h))
+
     down_hop(0, 0)
-    cf[...] = jnp.zeros_like(cf)
-    for j in range(lines):
-        grads = rg[j].reshape(rows, out_width)
-        cf[j, :, :rank_dim] = (adapter_scale * dot_nt(grads, bt[j])).astype(bf16)
+    for d in range(1, lines):
+        coef_back(d, 1).wait_recv()
     go(upper, coef_copy)
     down_hop(1, 0)
     a_step(1, 0)
@@ -414,17 +416,19 @@
     a_step(3, 1)
     project(2)
     project(3)
-    up_hop(0)
     down_hop(3, 1)
     down_hop(2, 2)
     term(3, 0)
-    up_hop(1)
     down_hop(3, 2)
     term(3, 1)
-    up_hop(2)
     for _, finish in downs:
         finish(gd)
-    up_finish(gu)
+    for d in range(1, lines):
+        other = (z + d) % lines
+        copy(pjs.at[other], pjr.at[other], p_s.at[d], p_r.at[other], seg, host(1)).wait_recv()
+    gu[...] = sum(
+        dot_nn(pjr[j, :, :rows], rg[j].reshape(rows, out_width)) for j in range(lines)
+    )
     for p in range(parts):
         for i in range(lines):
             for k in range(1, plane):
@@ -481,7 +485,8 @@
             pltpu.VMEM((chunks, lines, plane, cap, part), bf16),
             pltpu.VMEM((lines, plane, cap, out_width), bf16),
             pltpu.VMEM((parts, lines, 2 * rank_dim, wide), bf16),
-            pltpu.VMEM((lines, rank_dim, out_width), bf16),
+            pltpu.VMEM((lines, rows, lanes), bf16),
+            pltpu.VMEM((lines, rank_dim, lanes), bf16),
             pltpu.VMEM((lines, rows, lanes), bf16),
             pltpu.VMEM((lines, rank_dim, lanes), bf16),
             pltpu.VMEM((lines, rows, lanes), bf16),
@@ -489,18 +494,17 @@
             pltpu.VMEM((parts, plane, lines, cap, wide), bf16),
         ]
         + [pltpu.VMEM((chunks, lines, rank_dim, part), bf16)] * 4
-        + [pltpu.VMEM((lines, rank_dim, out_width), bf16)] * 4
+        + [pltpu.VMEM((lines, rank_dim, lanes), bf16)] * 2
         + [
-            pltpu.VMEM((lines, rank_dim, out_width), f32),
             dma((chunks, plane - 1)), dma((chunks, plane - 1)),
-            dma((plane - 1,)), dma((plane - 1,)),
+            dma((lines, plane)), dma((lines, plane)),
             dma((parts, 2, lines)), dma((parts, lines)),
-            dma((2, lines)), dma((lines,)),
             dma((parts, lines)), dma((parts, lines)),
             dma, dma,
             dma((parts, lines, plane - 1)), dma((parts, lines, plane - 1)),
             dma((chunks, 2, lines)), dma((chunks, 2, lines)),
             dma((2, lines)), dma((2, lines)),
+            dma((lines,)), dma((lines,)),
             dma((parts,)),
         ],
         compiler_params=pltpu.CompilerParams(

time: 83.5 us -> 82 us (0.982)
  Pallas kernels: 82.7 us -> 81.2 us
    pallas_call x1, Pallas kernels: 78.4 us -> 76.8 us  [local_lines(): pl.pallas_call(lines_kernel, out_shape=(jax.ShapeDtypeStruct((parts, plan...]
where the time goes in v6:
time: 82 us; the launch traced here: 81.8 us
  Pallas kernels  81.2 us (99%)
    pallas_call x1, Pallas kernels, local_lines(): pl.pallas_call(lines_kernel, out_shape=(jax.ShapeDtypeStruct((parts, plan...  76.8 us
    pallas_call x1, Pallas kernels, local_lines(): pl.pallas_call(select_kernel, grid=(tiles,), out_shape=(jax.ShapeDtypeStr...  4.32 us

profile of v6, /device:TPU:0, one launch (start us, length us, event | category | flops | bytes accessed | tf_op | source)
XLA Modules:
  0.0 81.8 jit_solution(7471913119454424787)
XLA Ops:
  0.6 76.8 %adapter_lines.1 = (bf16[2,4,4,16,2048]{4,3,2,1,0:T(8,128)(2,1)}, bf16[128,256]{1,0:T(8,128)(2,1)}, f32[64,4096]{1,0:T(8,128)}, f32[64,1024]{1,0:T(8,128)}) custom-call(bf16[128,4096]{1,0:T(8,128)(2,1)} %bitcast.15, bf16[128,1024]{1,0:T(8,128)(2,1)} %bitcast.17, s32[1,128]{1,0:T(1,128)} %bitcast.19, s32[1,16]{1,0:T(1,128)} %bitcast.20, ...), custom_call_target="tpu_custom_call" | custom-call | tf_op jit(solution)/shard_map/adapter_lines/pallas_call | solution.py:472
  77.5 4.3 %select_rows.1 = (bf16[128,4096]{1,0:T(8,128)(2,1)}, f32[64,4096]{1,0:T(8,128)}, f32[64,1024]{1,0:T(8,128)}) custom-call(bf16[2,256,2048]{2,1,0:T(8,128)(2,1)} %bitcast.14, bf16[128,256]{1,0:T(8,128)(2,1)} %get-tuple-element.11.back, f32[64,4096]{1,0:T(8,128)} %get-tuple-element.12.gd_in, f32[64,1024]{1,0:T(8,128)} %get-tuple-element.13.gu_in), custom_call_target="tpu_custom_call" | custom-call | tf_op jit(solution)/shard_map/select_rows/pallas_call | solution.py:527

commit v7 on v6

--- a/solution.py
+++ b/solution.py
@@ -443,10 +443,24 @@
             pl.when(cond)(functools.partial(lambda make: make().wait_send(), make))
 
 
-def select_kernel(returned, back, gd_in, gu_in, passed, gd, gu):
+def select_kernel(returned, back, gd_in, gu_in, passed, gd, gu, sems):
+    step = pl.program_id(0)
+    moves = [
+        pltpu.make_async_copy(gd_in, gd, sems.at[0]),
+        pltpu.make_async_copy(gu_in, gu, sems.at[1]),
+    ]
+
+    @pl.when(step == 0)
+    def _():
+        for move in moves:
+            move.start()
+
     passed[...] = dot_nn(back[...], returned[0]).astype(bf16)
-    gd[...] = gd_in[...]
-    gu[...] = gu_in[...]
+
+    @pl.when(step == pl.num_programs(0) - 1)
+    def _():
+        for move in moves:
+            move.wait()
 
 
 def local_lines(
@@ -522,8 +536,7 @@
     tiles = 4
     tile, each = width // tiles, tiles // parts
     columns = lambda c: (0, c)
-    down_spec = pl.BlockSpec((rank_dim, tile), columns)
-    up_spec = pl.BlockSpec((rank_dim, out_width // tiles), columns)
+    whole = pl.BlockSpec(memory_space=pl.ANY)
     passed, gd, gu = pl.pallas_call(
         select_kernel,
         grid=(tiles,),
@@ -535,10 +548,11 @@
         in_specs=[
             pl.BlockSpec((1, slots, tile), lambda c: (c // each, 0, c % each)),
             pl.BlockSpec((tok, slots), lambda c: (0, 0)),
-            down_spec,
-            up_spec,
+            whole,
+            whole,
         ],
-        out_specs=(pl.BlockSpec((tok, tile), columns), down_spec, up_spec),
+        out_specs=(pl.BlockSpec((tok, tile), columns), whole, whole),
+        scratch_shapes=[dma((2,))],
         compiler_params=pltpu.CompilerParams(vmem_limit_bytes=56 * 1024 * 1024),
         name="select_rows",
     )(returned.reshape(parts, slots, wide), back, gd, gu)

time: 82 us -> 120 us (1.46)
  Pallas kernels: 81.2 us -> 119 us
    pallas_call x1, Pallas kernels: 4.32 us -> 42.6 us  [local_lines(): pl.pallas_call(select_kernel, grid=(tiles,), out_shape=(jax.ShapeDtypeStr...]
where the time goes in v7:
time: 120 us
  Pallas kernels  119 us (99%)
    pallas_call x1, Pallas kernels, local_lines(): pl.pallas_call(lines_kernel, out_shape=(jax.ShapeDtypeStruct((parts, plan...  76.8 us
    pallas_call x1, Pallas kernels, local_lines(): pl.pallas_call(select_kernel, grid=(tiles,), out_shape=(jax.ShapeDtypeStr...  42.6 us

profile of v7, /device:TPU:0, one launch (start us, length us, event | category | flops | bytes accessed | tf_op | source)
XLA Modules:
  0.0 120.1 jit_solution(6445306080612054283)
XLA Ops:
  0.6 76.8 %adapter_lines.1 = (bf16[2,4,4,16,2048]{4,3,2,1,0:T(8,128)(2,1)}, bf16[128,256]{1,0:T(8,128)(2,1)}, f32[64,4096]{1,0:T(8,128)}, f32[64,1024]{1,0:T(8,128)}) custom-call(bf16[128,4096]{1,0:T(8,128)(2,1)} %bitcast.15, bf16[128,1024]{1,0:T(8,128)(2,1)} %bitcast.17, s32[1,128]{1,0:T(1,128)} %bitcast.19, s32[1,16]{1,0:T(1,128)} %bitcast.20, ...), custom_call_target="tpu_custom_call" | custom-call | tf_op jit(solution)/shard_map/adapter_lines/pallas_call | solution.py:486
  77.5 42.6 %select_rows.1 = (bf16[128,4096]{1,0:T(8,128)(2,1)}, f32[64,4096]{1,0:T(8,128)}, f32[64,1024]{1,0:T(8,128)}) custom-call(bf16[2,256,2048]{2,1,0:T(8,128)(2,1)} %bitcast.14, bf16[128,256]{1,0:T(8,128)(2,1)} %get-tuple-element.11.back, f32[64,4096]{1,0:T(8,128)} %get-tuple-element.12.gd_in, f32[64,1024]{1,0:T(8,128)} %get-tuple-element.13.gu_in), custom_call_target="tpu_custom_call" | custom-call | tf_op jit(solution)/shard_map/select_rows/pallas_call | solution.py:540
